TPU v7x, 32 devices: a whole 2x2x4 slice. The times are simulated.
32 devices in a mesh: groups: 2 (over x), tensor: 16 (over z, y, core).
Axes of the slice: x: 2, y: 2, z: 4, core: 2. Of those that a mesh axis runs over, the one named last changes fastest.
Arguments:
- hidden_in: bfloat16 [512, 5120], P(('groups', 'tensor')), parts along dimension 0, may hold values from -6 to 6
- norm_gain: float32 [5120], replicated, may hold values from 0.1 to 1.9
- w_gate: bfloat16 [5120, 17408], P(None, 'tensor'), may hold values from -0.078125 to 0.078125
- w_up: bfloat16 [5120, 17408], P(None, 'tensor'), may hold values from -0.078125 to 0.078125
- w_down: bfloat16 [17408, 5120], P('tensor'), may hold values from -0.046875 to 0.046875
- final_gain: float32 [5120], replicated, may hold values from 0.1 to 1.9
- adapter: bfloat16 [5120, 768], P('tensor'), may hold values from -0.078125 to 0.078125
- student_rows: bfloat16 [128, 768], P(('groups', 'tensor')), parts along dimension 0, may hold values from -6 to 6
- queries: float32 [32, 768], P(('groups', 'tensor')), parts along dimension 0, may hold values from -6 to 6
- doc_list: int32 [128], P(('groups', 'tensor')), parts along dimension 0, may hold values from 0 to 15, as said below
- teacher_rank: int32 [128], P(('groups', 'tensor')), parts along dimension 0, may hold values from 0 to 15, as said below
Outputs:
- teacher_rows: bfloat16 [128, 5120], P(('groups', 'tensor')), parts along dimension 0
- grad_rows: float32 [128, 768], P(('groups', 'tensor')), parts along dimension 0
- grad_queries: float32 [32, 768], P(('groups', 'tensor')), parts along dimension 0
- list_losses: float32 [32], P(('groups', 'tensor')), parts along dimension 0
There are 2 independent parts, one for each index of `groups`. A program takes and returns all parts, laid end to end along the dimension named above; an argument that names none is the same for every part. Nothing has to cross between parts.
Inputs may be any that keep to these rules, and one draw needn't show every extreme that they name: `doc_list`: every list holds 1 to 16 documents and one list exactly 16. `teacher_rank`: within each list the ranks of its documents are 0 to its length minus 1, each once.
All inputs are finite; a program needn't handle non-finite values.
Results may differ from a plain program's by a relative error of at most 0.0051.
Values may be sent and summed in bfloat16 or wider, within the bound.
A program may use at most 128 MiB of HBM per device.

v0:
```python
import math

import jax
import jax.numpy as jnp
from jax import lax
from jax.experimental import pallas as pl
from jax.experimental.pallas import tpu as pltpu
from jax.sharding import PartitionSpec as P

SEQ = 4


EPSILON = 1e-06
SOFTMAX_HEAT = 0.5


def list_losses_of(score_values, member, rank_f):
    pairwise_terms = jnp.dot(member, member.T, precision=lax.Precision.HIGHEST)
    pairwise_terms = pairwise_terms * (
        1.0 - jnp.eye(score_values.shape[0], dtype=score_values.dtype)
    )
    outranked_count = pairwise_terms * jax.nn.sigmoid(
        (score_values[None, :] - score_values[:, None]) / SOFTMAX_HEAT
    )
    approx_rank = 1.0 + jnp.sum(outranked_count, axis=1)
    gains = 1.0 / jnp.log2(2.0 + rank_f)
    earned = jnp.dot(member.T, gains / jnp.log2(1.0 + approx_rank), precision=lax.Precision.HIGHEST)
    ideal = jnp.dot(member.T, gains * gains, precision=lax.Precision.HIGHEST)
    return 1.0 - earned / ideal


def local(
    hidden_in,
    norm_gain,
    w_gate,
    w_up,
    w_down,
    final_gain,
    adapter,
    student_rows,
    queries,
    doc_list,
    teacher_rank,
):
    list_entries = lax.axis_size("tensor")
    my_index = lax.axis_index("tensor")
    tokens_f = hidden_in.astype(jnp.float32)
    normed = (
        tokens_f
        * lax.rsqrt(jnp.mean(tokens_f * tokens_f, axis=-1, keepdims=True) + EPSILON)
        * norm_gain
    ).astype(jnp.bfloat16)
    shard_rows = lax.all_gather(normed, "tensor", axis=0, tiled=True)
    gate_out = jnp.dot(shard_rows, w_gate, preferred_element_type=jnp.float32)
    up_out = jnp.dot(shard_rows, w_up, preferred_element_type=jnp.float32)
    hidden = (jax.nn.silu(gate_out) * up_out).astype(jnp.bfloat16)
    doc_rows = hidden_in.shape[0] // SEQ
    mixed = jnp.dot(hidden, w_down, preferred_element_type=jnp.float32)
    pooled_mix = lax.psum_scatter(
        mixed.reshape(lax.axis_size("tensor") * doc_rows, SEQ, mixed.shape[1]).mean(axis=1),
        "tensor",
        scatter_dimension=0,
        tiled=True,
    )
    pooled = pooled_mix + tokens_f.reshape(doc_rows, SEQ, tokens_f.shape[1]).mean(axis=1)
    normed_rows = (
        pooled * lax.rsqrt(jnp.mean(pooled * pooled, axis=-1, keepdims=True) + EPSILON) * final_gain
    )
    teacher_rows = normed_rows.astype(jnp.bfloat16)
    student_width = adapter.shape[1]
    target = jnp.dot(
        teacher_rows,
        lax.all_gather(adapter, "tensor", axis=0, tiled=True),
        preferred_element_type=jnp.float32,
    )
    rows_f = student_rows.astype(jnp.float32)
    residual = rows_f - target
    scale_root = math.sqrt(student_width)
    list_ids = jnp.arange(list_entries, dtype=jnp.int32)
    own_member = doc_list[:, None] == list_ids[None, :]
    query_all = lax.all_gather(queries, "tensor", axis=0, tiled=True)
    own_onehot = own_member.astype(jnp.float32)
    chosen = jnp.dot(own_onehot, query_all, precision=lax.Precision.HIGHEST)
    own_scores = jnp.sum(rows_f * chosen, axis=1) / scale_root
    all_scores = lax.all_gather(own_scores, "tensor", axis=0, tiled=True)
    all_lists, all_ranks = (
        lax.all_gather(doc_list, "tensor", axis=0, tiled=True),
        lax.all_gather(teacher_rank, "tensor", axis=0, tiled=True),
    )
    member = (all_lists[:, None] == list_ids[None, :]).astype(jnp.float32)
    rank_f = all_ranks.astype(jnp.float32)
    per_list, pullback = jax.vjp(lambda values: list_losses_of(values, member, rank_f), all_scores)
    score_grad = pullback(jnp.full(per_list.shape, float(student_width), jnp.float32))[0]
    own_grad = lax.dynamic_slice_in_dim(score_grad, my_index * doc_rows, doc_rows, 0)
    grad_rows = own_grad[:, None] * chosen / scale_root + residual
    query_terms = (
        jnp.dot(own_onehot.T, own_grad[:, None] * rows_f, precision=lax.Precision.HIGHEST)
        / scale_root
    )
    grad_queries = lax.psum_scatter(query_terms, "tensor", scatter_dimension=0, tiled=True)
    own_losses = lax.dynamic_slice_in_dim(per_list, my_index, 1, 0)
    return (teacher_rows, grad_rows, grad_queries, own_losses)


CHIPS = 8
COLS = 640
HALF = 2560
FIRST = 160
F32 = jnp.float32
BF16 = jnp.bfloat16


def chip_at(pos):
    y = pos // 4
    return 2 * (pos + y * (7 - 2 * pos)) + y


def pos_of(chip):
    y = chip % 2
    z = chip // 2
    return z + y * (7 - 2 * z)


def slot_of(rel):
    return 2 * rel if rel < 4 else 15 - 2 * rel


def slot_vec(chip, p):
    y = chip & 1
    z = chip >> 1
    rel = (z + y * (7 - 2 * z) - p + 8) & 7
    return jnp.where(rel < 4, 2 * rel, 15 - 2 * rel)


def kernel(
    hin, ngain, wg_hbm, wu_hbm, wd_hbm, fgain, ad_hbm, student, query, lists, ranks,
    out_rows, out_grad, out_query, out_loss,
    xraw, xn, wg, wu, wd, ad, hid, part, sib_out, sib_in, rs_r_out, rs_r_in, rs_l_out, rs_l_in,
    fin_out, fin, small, gvec,
    w_sem, ag_rs, ag_rr, ag_ls, ag_lr, ag_ss, ag_sr, ad_sem, sm_s, sm_r, sms_s, sms_r,
    sb_s, sb_r, rr_s, rr_r, rl_s, rl_r, fi_s, fi_r,
):
    t = lax.axis_index("tensor")
    c = t % 2
    chip = t // 2
    p = pos_of(chip)

    def plane(rel):
        return chip_at((p + rel) % CHIPS) * 2 + c

    right, left, sibling = plane(1), plane(7), chip * 2 + (1 - c)
    sent = []

    def remote(src, dst, ssem, rsem, dev):
        return pltpu.make_async_remote_copy(
            src_ref=src, dst_ref=dst, send_sem=ssem, recv_sem=rsem,
            device_id={"tensor": dev}, device_id_type=pl.DeviceIdType.MESH,
        )

    def go(copy):
        copy.start()
        sent.append(copy)
        return copy

    barrier = pltpu.get_barrier_semaphore()
    for rel in range(1, CHIPS):
        pl.semaphore_signal(barrier, inc=1, device_id={"tensor": plane(rel)}, device_id_type=pl.DeviceIdType.MESH)
    pl.semaphore_signal(barrier, inc=1, device_id={"tensor": sibling}, device_id_type=pl.DeviceIdType.MESH)

    loads = []
    for i, (src, dst) in enumerate(((wg_hbm, wg), (wu_hbm, wu), (wd_hbm, wd))):
        rows = src.shape[0] // 4
        for j in range(4):
            copy = pltpu.make_async_copy(src.at[pl.ds(j * rows, rows)], dst.at[pl.ds(j * rows, rows)], w_sem.at[i, j])
            copy.start()
            loads.append(copy)
    ad_rows = pl.ds(pl.multiple_of(c * 320, 64), 320)
    ad_local = pltpu.make_async_copy(ad_hbm, ad.at[ad_rows], ad_sem.at[0])
    ad_local.start()
    pl.semaphore_wait(barrier, CHIPS)

    def block(slot, half):
        return pl.ds((slot * 2 + half) * 16, 16)

    def cols(h):
        return pl.ds(h * HALF, HALF)

    def hop(step, h, to_right):
        if to_right:
            src_slot = 0 if step == 0 else 2 * step - 1
            dst_slot = 2 * step + 1
            ssem, rsem, dev = ag_rs.at[step, h], ag_rr.at[step, h], right
        else:
            src_slot = 2 * step
            dst_slot = 2 * step + 2 if step < 3 else 7
            ssem, rsem, dev = ag_ls.at[step, h], ag_lr.at[step, h], left
        src = hin.at[:, cols(h)] if step == 0 else xraw.at[block(src_slot, 0), cols(h)]
        return remote(src, xraw.at[block(dst_slot, 0), cols(h)], ssem, rsem, dev)

    def share(slot, h):
        src = hin.at[:, cols(h)] if slot == 0 else xraw.at[block(slot, 0), cols(h)]
        return remote(src, xraw.at[block(slot, 1), cols(h)], ag_ss.at[slot, h], ag_sr.at[slot, h], sibling)

    hops = {}
    shares = {}
    for h in range(2):
        hops[0, h, True] = go(hop(0, h, True))
        hops[0, h, False] = go(hop(0, 1 - h, False))
    hops[0, 0, False], hops[0, 1, False] = hops[0, 1, False], hops[0, 0, False]
    for h in range(2):
        shares[0, h] = go(share(0, h))
    ad_remote = go(remote(ad_hbm, ad.at[ad_rows], ad_sem.at[1], ad_sem.at[2], sibling))

    small[0, 0:4, 0:768] = student[...].astype(F32)
    small[0, 4:5, 0:768] = query[...]
    row8 = lax.broadcasted_iota(jnp.int32, (8, 128), 0)
    lane8 = lax.broadcasted_iota(jnp.int32, (8, 128), 1)
    meta = jnp.zeros((8, 128), F32)
    for i in range(4):
        meta = jnp.where((row8 == i) & (lane8 == 0), lists[i].astype(F32), meta)
        meta = jnp.where((row8 == i) & (lane8 == 1), ranks[i].astype(F32), meta)
    small[0, 5:8, 0:768] = jnp.zeros((3, 768), F32)
    small[0, :, 768:896] = meta

    def normalise(slot, half):
        rows = block(slot, half)
        values = xraw[rows, :].astype(F32)
        scale = lax.rsqrt(jnp.mean(values * values, axis=-1, keepdims=True) + EPSILON)
        xn[rows, :] = (values * scale * ngain[...]).astype(BF16)

    xraw[0:16, :] = hin[...]
    normalise(0, 0)

    def shared(slot):
        for h in range(2):
            shares[slot, h].wait_recv()
        normalise(slot, 1)

    def gate_tile(first, rows, tile, width):
        x = xn[pl.ds(first, rows), :]
        gate = jnp.dot(x, wg[:, pl.ds(tile, width)], preferred_element_type=F32)
        up = jnp.dot(x, wu[:, pl.ds(tile, width)], preferred_element_type=F32)
        hid[pl.ds(first, rows), pl.ds(tile, width)] = (gate * jax.nn.sigmoid(gate) * up).astype(BF16)

    def hidden_rows(first, rows, width):
        whole = width // 256

        def body(i, carry):
            gate_tile(first, rows, pl.multiple_of(i * 256, 256), 256)
            return carry

        lax.fori_loop(0, whole, body, 0)
        if width % 256:
            gate_tile(first, rows, whole * 256, width % 256)

    units = wg.shape[1]
    for step in range(4):
        for k in range(2):
            for to_right in (True, False):
                h = k if to_right else 1 - k
                if step == 3 and k == 1:
                    continue
                hops[step, h, to_right].wait_recv()
                slot = 7 if step == 3 else (2 * step + 1 if to_right else 2 * step + 2)
                if step < 2 or (step == 2 and k == 0):
                    hops[step + 1, h, to_right] = go(hop(step + 1, h, to_right))
                shares[slot, h] = go(share(slot, h))
        if step == 0:
            shared(0)
            normalise(1, 0)
            normalise(2, 0)
        elif step == 1:
            shared(1)
            shared(2)
            normalise(3, 0)
            normalise(4, 0)
            shared(3)
            shared(4)
            for copy in loads[:8]:
                copy.wait()
        elif step == 2:
            normalise(5, 0)
            normalise(6, 0)
            shared(5)
            shared(6)
    hidden_rows(0, FIRST, units)
    normalise(7, 0)
    shared(7)

    small_copies = {}
    for rel in range(1, CHIPS):
        dst = slot_of(8 - rel)
        small_copies[8 - rel] = go(remote(small.at[0], small.at[2 * dst], sm_s.at[rel], sm_r.at[8 - rel], plane(rel)))
    small_shares = {0: go(remote(small.at[0], small.at[1], sms_s.at[0], sms_r.at[0], sibling))}

    hidden_rows(FIRST, 256 - FIRST, units)

    for rel in range(1, CHIPS):
        small_copies[rel].wait_recv()
        slot = slot_of(rel)
        small_shares[slot] = go(remote(small.at[2 * slot], small.at[2 * slot + 1], sms_s.at[slot], sms_r.at[slot], sibling))

    doc = lax.broadcasted_iota(jnp.int32, (64, 256), 0)
    token = lax.broadcasted_iota(jnp.int32, (64, 256), 1)
    place = (slot_vec((doc & 31) >> 2, p) * 2 + (doc >> 5)) * 4 + (doc & 3)
    pool = jnp.where((token >> 2) == place, 0.25, 0.0).astype(BF16)
    pooled_hidden = jnp.dot(pool, hid[...], preferred_element_type=F32).astype(BF16)
    for copy in loads[8:]:
        copy.wait()

    def columns(rel):
        return pl.ds(pl.multiple_of(chip_at((p + rel) % CHIPS) * COLS, 128), COLS)

    sibs = {}

    def down(rel):
        mixed = jnp.dot(pooled_hidden, wd[:, columns(rel)], preferred_element_type=F32)
        part[rel] = mixed[0:32]
        sib_out[rel] = mixed[32:64]
        sibs[rel] = go(remote(sib_out.at[rel], sib_in.at[rel], sb_s.at[rel], sb_r.at[rel], sibling))

    def mine(rel):
        sibs[rel].wait_recv()
        return part[rel] + sib_in[rel]

    rights, lefts = {}, {}

    def send_right(step):
        total = mine(4 - step)
        if step:
            rights[step - 1].wait_recv()
            total = total + rs_r_in[step - 1].astype(F32)
        rs_r_out[step] = total.astype(BF16)
        rights[step] = go(remote(rs_r_out.at[step], rs_r_in.at[step], rr_s.at[step], rr_r.at[step], right))

    def send_left(step):
        total = mine(5 + step)
        if step:
            lefts[step - 1].wait_recv()
            total = total + rs_l_in[step - 1].astype(F32)
        rs_l_out[step] = total.astype(BF16)
        lefts[step] = go(remote(rs_l_out.at[step], rs_l_in.at[step], rl_s.at[step], rl_r.at[step], left))

    down(4)
    down(5)
    send_right(0)
    send_left(0)
    down(3)
    down(6)
    send_right(1)
    send_left(1)
    down(2)
    down(7)
    send_right(2)
    send_left(2)
    down(1)
    down(0)
    own_cols = columns(0)
    pooled_in = jnp.dot(pool[0:32], xraw[:, own_cols], preferred_element_type=F32)
    send_right(3)

    for slot in range(CHIPS):
        small_shares[slot].wait_recv()
    table = small[:, :, 0:768].reshape(128, 768)
    metas = small[:, :, 768:896].reshape(128, 128)
    row = lax.broadcasted_iota(jnp.int32, (128, 128), 0)
    lane = lax.broadcasted_iota(jnp.int32, (128, 128), 1)
    list_c = jnp.broadcast_to(metas[:, 0:1], (128, 128))
    rank_c = metas[:, 1:2]
    list_r = list_c.T
    doc_c = (row & 7) < 4
    doc_r = (lane & 7) < 4

    def query_place(list_f):
        ids = list_f.astype(jnp.int32)
        half = (ids & 1) ^ c
        return (slot_vec(ids >> 1, p) * 2 + half) * 8 + 4

    highest = lax.Precision.HIGHEST
    grams = lax.dot_general(table, table, (((1,), (1,)), ((), ())), precision=highest, preferred_element_type=F32)
    chosen_hot = jnp.where(doc_c & (lane == query_place(list_c)), 1.0, 0.0)
    root = math.sqrt(768)
    score_c = jnp.broadcast_to(jnp.sum(grams * chosen_hot, axis=1, keepdims=True) / root, (128, 128))
    same = doc_c & doc_r & (list_c == list_r)
    pair = jnp.where(same & (row != lane), 1.0, 0.0)
    sig = jax.nn.sigmoid((score_c.T - score_c) / SOFTMAX_HEAT)
    approx = 1.0 + jnp.sum(pair * sig, axis=1, keepdims=True)
    ln2 = math.log(2.0)
    gains = ln2 / jnp.log(2.0 + rank_c)
    gains_b = jnp.broadcast_to(gains * gains, (128, 128))
    ideal = jnp.sum(jnp.where(same, gains_b.T, 0.0), axis=1, keepdims=True)
    ideal = jnp.where(ideal > 0.0, ideal, 1.0)
    log_a = jnp.log(1.0 + approx) / ln2
    weight = 768.0 * gains / (ideal * log_a * log_a * (1.0 + approx) * ln2)
    weight_b = jnp.broadcast_to(weight, (128, 128))
    pull = pair * sig * (1.0 - sig) / SOFTMAX_HEAT
    grad_c = jnp.broadcast_to(jnp.sum(pull * (weight_b.T - weight_b), axis=1, keepdims=True), (128, 128))
    gvec[...] = grad_c
    hot8 = chosen_hot[0:8]
    chosen = jnp.dot(hot8, table, precision=highest, preferred_element_type=F32)
    grad_r = jnp.where(doc_r & (list_r == t.astype(F32)), grad_c.T, 0.0)[0:8]
    out_query[...] = jnp.dot(grad_r, table, precision=highest, preferred_element_type=F32)[0:1] / root
    in_list = doc_c & (list_c == t.astype(F32))
    earned = jnp.sum(jnp.where(in_list, gains / log_a, 0.0), axis=0, keepdims=True)
    best = jnp.sum(jnp.where(in_list, gains_b, 0.0), axis=0, keepdims=True)
    out_loss[...] = 1.0 - earned / best
    score_part = gvec[0:4, 0:1] * chosen[0:4] / root + small[0, 0:4, 0:768]

    ad_local.wait()
    ad_remote.wait_recv()
    lefts[2].wait_recv()
    rights[3].wait_recv()
    pooled = mine(0) + rs_l_in[2].astype(F32) + rs_r_in[3].astype(F32) + pooled_in
    scaled = pooled * fgain[:, own_cols]
    high = scaled.astype(BF16)
    low = (scaled - high.astype(F32)).astype(BF16)
    both = jnp.dot(jnp.concatenate([high, low], axis=0), ad[...], preferred_element_type=F32)
    product = both[0:32] + both[32:64]
    for q in range(CHIPS):
        fin_out[q, :, 0:COLS] = pooled[4 * q : 4 * q + 4]
        fin_out[q, :, COLS:1408] = product[4 * q : 4 * q + 4]
    finals = []
    for rel in range(1, CHIPS):
        finals.append(
            go(remote(fin_out.at[chip_at((p + rel) % CHIPS)], fin.at[chip], fi_s.at[rel], fi_r.at[8 - rel], plane(rel)))
        )
    fin[chip] = fin_out[chip]
    for copy in finals:
        copy.wait_recv()
    rows = jnp.concatenate([fin[q, :, 0:COLS] for q in range(CHIPS)], axis=1)
    scale = lax.rsqrt(jnp.mean(rows * rows, axis=-1, keepdims=True) + EPSILON)
    out_rows[...] = (rows * scale * fgain[...]).astype(BF16)
    target = fin[0, :, COLS:1408]
    for q in range(1, CHIPS):
        target = target + fin[q, :, COLS:1408]
    out_grad[...] = score_part - target * scale
    for copy in sent:
        copy.wait_send()


def fused(hidden_in, norm_gain, w_gate, w_up, w_down, final_gain, adapter, student_rows, queries, doc_list, teacher_rank):
    units = w_gate.shape[1]
    dma = pltpu.SemaphoreType.DMA
    vmem = pl.BlockSpec(memory_space=pltpu.VMEM)
    smem = pl.BlockSpec(memory_space=pltpu.SMEM)
    hbm = pl.BlockSpec(memory_space=pl.ANY)
    rows, grad, query, loss = pl.pallas_call(
        kernel,
        out_shape=(
            jax.ShapeDtypeStruct((4, 5120), BF16),
            jax.ShapeDtypeStruct((4, 768), F32),
            jax.ShapeDtypeStruct((1, 768), F32),
            jax.ShapeDtypeStruct((1, 128), F32),
        ),
        in_specs=[vmem, vmem, hbm, hbm, hbm, vmem, hbm, vmem, vmem, smem, smem],
        out_specs=(vmem, vmem, vmem, vmem),
        scratch_shapes=[
            pltpu.VMEM((256, 5120), BF16),
            pltpu.VMEM((256, 5120), BF16),
            pltpu.VMEM((5120, units), BF16),
            pltpu.VMEM((5120, units), BF16),
            pltpu.VMEM((units, 5120), BF16),
            pltpu.VMEM((640, 768), BF16),
            pltpu.VMEM((256, units), BF16),
            pltpu.VMEM((CHIPS, 32, COLS), F32),
            pltpu.VMEM((CHIPS, 32, COLS), F32),
            pltpu.VMEM((CHIPS, 32, COLS), F32),
            pltpu.VMEM((4, 32, COLS), BF16),
            pltpu.VMEM((4, 32, COLS), BF16),
            pltpu.VMEM((3, 32, COLS), BF16),
            pltpu.VMEM((3, 32, COLS), BF16),
            pltpu.VMEM((CHIPS, 4, 1408), F32),
            pltpu.VMEM((CHIPS, 4, 1408), F32),
            pltpu.VMEM((16, 8, 896), F32),
            pltpu.VMEM((128, 128), F32),
            dma((3, 4)),
            dma((4, 2)),
            dma((4, 2)),
            dma((4, 2)),
            dma((4, 2)),
            dma((8, 2)),
            dma((8, 2)),
            dma((3,)),
            dma((8,)),
            dma((8,)),
            dma((8,)),
            dma((8,)),
            dma((8,)),
            dma((8,)),
            dma((4,)),
            dma((4,)),
            dma((3,)),
            dma((3,)),
            dma((8,)),
            dma((8,)),
        ],
        compiler_params=pltpu.CompilerParams(
            collective_id=0, has_side_effects=True, vmem_limit_bytes=58 * 1024 * 1024
        ),
        cost_estimate=pl.CostEstimate(flops=8_000_000_000, bytes_accessed=34_000_000, transcendentals=300_000),
    )(
        hidden_in, norm_gain[None, :], w_gate, w_up, w_down, final_gain[None, :], adapter,
        student_rows, queries, doc_list, teacher_rank,
    )
    return rows, grad, query, loss[0, 0:1]


def solution(mesh):
    placed = (
        P(("groups", "tensor"), None),
        P(),
        P(None, "tensor"),
        P(None, "tensor"),
        P("tensor", None),
        P(),
        P("tensor", None),
        P(("groups", "tensor"), None),
        P(("groups", "tensor"), None),
        P(("groups", "tensor")),
        P(("groups", "tensor")),
    )
    return jax.shard_map(
        fused if mesh.shape["tensor"] == 2 * CHIPS else local,
        mesh=mesh,
        in_specs=placed,
        out_specs=(
            P(("groups", "tensor"), None),
            P(("groups", "tensor"), None),
            P(("groups", "tensor"), None),
            P(("groups", "tensor")),
        ),
        check_vma=False,
    )
```

profile of v0, /device:TPU:0, one launch (start us, length us, event | category | flops | bytes accessed | tf_op | source)
XLA Modules:
  0.0 91.4 jit_solution(9641428379172134410)
XLA Ops:
  0.6 14.7 %copy.15.wg_hbm = bf16[5120,1088]{1,0:T(8,128)(2,1)} copy(bf16[5120,1088]{0,1:T(8,128)(2,1)} %param.13) | data formatting | bytes 22282240 | tf_op args[2]
  15.3 14.6 %copy.16.wu_hbm = bf16[5120,1088]{1,0:T(8,128)(2,1)} copy(bf16[5120,1088]{0,1:T(8,128)(2,1)} %param.14) | data formatting | bytes 22282240 | tf_op args[3]
  29.9 55.7 %shard_map.138 = (bf16[4,5120]{1,0:T(4,128)(2,1)}, f32[4,768]{1,0:T(4,128)}, f32[1,768]{1,0:T(1,128)}, f32[1,128]{1,0:T(1,128)}) custom-call(bf16[16,5120]{1,0:T(8,128)(2,1)} %hin.1, f32[1,5120]{1,0:T(1,128)} %bitcast.4, bf16[5120,1088]{1,0:T(8,128)(2,1)} %copy.15.wg_hbm, bf16[5120,1088]{1,0:T(8,128)(2,1)} %copy.16.wu_hbm, bf16[1088,5120]{1,0:T(8,128)(2,1)} %wd_hbm.1, ...), custom_call_target="tpu_custom_call" | custom-call | flops 8000000000 | bytes 34000000 | tf_op jit(solution)/shard_map/pallas_call | solution.py:447
  85.7 1.4 %copy.21 = bf16[4,5120]{1,0:T(4,128)(2,1)} copy(bf16[4,5120]{1,0:T(4,128)(2,1)} %get-tuple-element.16) | data formatting | bytes 81920
  87.1 1.3 %copy.22 = f32[4,768]{1,0:T(4,128)} copy(f32[4,768]{1,0:T(4,128)} %get-tuple-element.17) | data formatting | bytes 24576
  88.4 1.3 %copy.23 = f32[1,768]{1,0:T(1,128)} copy(f32[1,768]{1,0:T(1,128)} %get-tuple-element.18) | data formatting | bytes 6144
where the time goes:
time: 92.4 us; the launch traced here: 91.4 us
  Pallas kernels  55.7 us (60%)
  local copies, waits for them, and re-layouts  33.3 us (36%)
  between operations  2.41 us (3%)
    pallas_call x1, Pallas kernels, fused(): pl.pallas_call(kernel, out_shape=(jax.ShapeDtypeStruct((4, 5120), BF16),...  55.7 us
    unnamed x5, local copies, waits for them, and re-layouts  33.3 us

commit v1 on v0

--- a/solution.py
+++ b/solution.py
@@ -167,13 +167,17 @@
         pl.semaphore_signal(barrier, inc=1, device_id={"tensor": plane(rel)}, device_id_type=pl.DeviceIdType.MESH)
     pl.semaphore_signal(barrier, inc=1, device_id={"tensor": sibling}, device_id_type=pl.DeviceIdType.MESH)
 
-    loads = []
+    units = wg.shape[0]
+    tiles = [(at, min(256, units - at)) for at in range(0, units, 256)]
+    loads = {}
     for i, (src, dst) in enumerate(((wg_hbm, wg), (wu_hbm, wu), (wd_hbm, wd))):
-        rows = src.shape[0] // 4
-        for j in range(4):
-            copy = pltpu.make_async_copy(src.at[pl.ds(j * rows, rows)], dst.at[pl.ds(j * rows, rows)], w_sem.at[i, j])
-            copy.start()
-            loads.append(copy)
+        for j, tile in enumerate(tiles):
+            loads[i, j] = pltpu.make_async_copy(src.at[pl.ds(*tile)], dst.at[pl.ds(*tile)], w_sem.at[i, j])
+    for j in range(len(tiles)):
+        loads[0, j].start()
+        loads[1, j].start()
+    for j in range(len(tiles)):
+        loads[2, j].start()
     ad_rows = pl.ds(pl.multiple_of(c * 320, 64), 320)
     ad_local = pltpu.make_async_copy(ad_hbm, ad.at[ad_rows], ad_sem.at[0])
     ad_local.start()
@@ -236,24 +240,31 @@
             shares[slot, h].wait_recv()
         normalise(slot, 1)
 
-    def gate_tile(first, rows, tile, width):
+    def gate_tile(first, rows, at, width):
         x = xn[pl.ds(first, rows), :]
-        gate = jnp.dot(x, wg[:, pl.ds(tile, width)], preferred_element_type=F32)
-        up = jnp.dot(x, wu[:, pl.ds(tile, width)], preferred_element_type=F32)
-        hid[pl.ds(first, rows), pl.ds(tile, width)] = (gate * jax.nn.sigmoid(gate) * up).astype(BF16)
-
-    def hidden_rows(first, rows, width):
-        whole = width // 256
+        dims = (((1,), (1,)), ((), ()))
+        gate = lax.dot_general(x, wg[pl.ds(at, width), :], dims, preferred_element_type=F32)
+        up = lax.dot_general(x, wu[pl.ds(at, width), :], dims, preferred_element_type=F32)
+        hid[pl.ds(first, rows), pl.ds(at, width)] = (gate * jax.nn.sigmoid(gate) * up).astype(BF16)
+
+    def early(*which):
+        for j in which:
+            if j < len(tiles):
+                loads[0, j].wait()
+                loads[1, j].wait()
+                gate_tile(0, FIRST, *tiles[j])
+
+    def hidden_rows(first, rows):
+        whole = units // 256
 
         def body(i, carry):
             gate_tile(first, rows, pl.multiple_of(i * 256, 256), 256)
             return carry
 
         lax.fori_loop(0, whole, body, 0)
-        if width % 256:
-            gate_tile(first, rows, whole * 256, width % 256)
-
-    units = wg.shape[1]
+        if units % 256:
+            gate_tile(first, rows, whole * 256, units % 256)
+
     for step in range(4):
         for k in range(2):
             for to_right in (True, False):
@@ -265,6 +276,8 @@
                 if step < 2 or (step == 2 and k == 0):
                     hops[step + 1, h, to_right] = go(hop(step + 1, h, to_right))
                 shares[slot, h] = go(share(slot, h))
+            if step == 2 and k == 0:
+                early(1, 2)
         if step == 0:
             shared(0)
             normalise(1, 0)
@@ -276,14 +289,14 @@
             normalise(4, 0)
             shared(3)
             shared(4)
-            for copy in loads[:8]:
-                copy.wait()
+            early(0)
         elif step == 2:
             normalise(5, 0)
             normalise(6, 0)
+            early(3)
             shared(5)
             shared(6)
-    hidden_rows(0, FIRST, units)
+    early(*range(4, len(tiles)))
     normalise(7, 0)
     shared(7)
 
@@ -293,7 +306,7 @@
         small_copies[8 - rel] = go(remote(small.at[0], small.at[2 * dst], sm_s.at[rel], sm_r.at[8 - rel], plane(rel)))
     small_shares = {0: go(remote(small.at[0], small.at[1], sms_s.at[0], sms_r.at[0], sibling))}
 
-    hidden_rows(FIRST, 256 - FIRST, units)
+    hidden_rows(FIRST, 256 - FIRST)
 
     for rel in range(1, CHIPS):
         small_copies[rel].wait_recv()
@@ -305,8 +318,8 @@
     place = (slot_vec((doc & 31) >> 2, p) * 2 + (doc >> 5)) * 4 + (doc & 3)
     pool = jnp.where((token >> 2) == place, 0.25, 0.0).astype(BF16)
     pooled_hidden = jnp.dot(pool, hid[...], preferred_element_type=F32).astype(BF16)
-    for copy in loads[8:]:
-        copy.wait()
+    for j in range(len(tiles)):
+        loads[2, j].wait()
 
     def columns(rel):
         return pl.ds(pl.multiple_of(chip_at((p + rel) % CHIPS) * COLS, 128), COLS)
@@ -347,17 +360,6 @@
     send_left(0)
     down(3)
     down(6)
-    send_right(1)
-    send_left(1)
-    down(2)
-    down(7)
-    send_right(2)
-    send_left(2)
-    down(1)
-    down(0)
-    own_cols = columns(0)
-    pooled_in = jnp.dot(pool[0:32], xraw[:, own_cols], preferred_element_type=F32)
-    send_right(3)
 
     for slot in range(CHIPS):
         small_shares[slot].wait_recv()
@@ -378,6 +380,12 @@
 
     highest = lax.Precision.HIGHEST
     grams = lax.dot_general(table, table, (((1,), (1,)), ((), ())), precision=highest, preferred_element_type=F32)
+
+    send_right(1)
+    send_left(1)
+    down(2)
+    down(7)
+
     chosen_hot = jnp.where(doc_c & (lane == query_place(list_c)), 1.0, 0.0)
     root = math.sqrt(768)
     score_c = jnp.broadcast_to(jnp.sum(grams * chosen_hot, axis=1, keepdims=True) / root, (128, 128))
@@ -396,6 +404,13 @@
     pull = pair * sig * (1.0 - sig) / SOFTMAX_HEAT
     grad_c = jnp.broadcast_to(jnp.sum(pull * (weight_b.T - weight_b), axis=1, keepdims=True), (128, 128))
     gvec[...] = grad_c
+
+    send_right(2)
+    send_left(2)
+    down(1)
+    down(0)
+    own_cols = columns(0)
+    pooled_in = jnp.dot(pool[0:32], xraw[:, own_cols], preferred_element_type=F32)
     hot8 = chosen_hot[0:8]
     chosen = jnp.dot(hot8, table, precision=highest, preferred_element_type=F32)
     grad_r = jnp.where(doc_r & (list_r == t.astype(F32)), grad_c.T, 0.0)[0:8]
@@ -405,6 +420,7 @@
     best = jnp.sum(jnp.where(in_list, gains_b, 0.0), axis=0, keepdims=True)
     out_loss[...] = 1.0 - earned / best
     score_part = gvec[0:4, 0:1] * chosen[0:4] / root + small[0, 0:4, 0:768]
+    send_right(3)
 
     ad_local.wait()
     ad_remote.wait_recv()
@@ -438,6 +454,13 @@
         copy.wait_send()
 
 
+def hand_over(rows, grad, query, loss, out_rows, out_grad, out_query, out_loss):
+    out_rows[...] = rows[...]
+    out_grad[...] = grad[...]
+    out_query[...] = query[...]
+    out_loss[0] = loss[0, 0]
+
+
 def fused(hidden_in, norm_gain, w_gate, w_up, w_down, final_gain, adapter, student_rows, queries, doc_list, teacher_rank):
     units = w_gate.shape[1]
     dma = pltpu.SemaphoreType.DMA
@@ -457,8 +480,8 @@
         scratch_shapes=[
             pltpu.VMEM((256, 5120), BF16),
             pltpu.VMEM((256, 5120), BF16),
-            pltpu.VMEM((5120, units), BF16),
-            pltpu.VMEM((5120, units), BF16),
+            pltpu.VMEM((units, 5120), BF16),
+            pltpu.VMEM((units, 5120), BF16),
             pltpu.VMEM((units, 5120), BF16),
             pltpu.VMEM((640, 768), BF16),
             pltpu.VMEM((256, units), BF16),
@@ -473,7 +496,7 @@
             pltpu.VMEM((CHIPS, 4, 1408), F32),
             pltpu.VMEM((16, 8, 896), F32),
             pltpu.VMEM((128, 128), F32),
-            dma((3, 4)),
+            dma((3, pl.cdiv(units, 256))),
             dma((4, 2)),
             dma((4, 2)),
             dma((4, 2)),
@@ -499,10 +522,20 @@
         ),
         cost_estimate=pl.CostEstimate(flops=8_000_000_000, bytes_accessed=34_000_000, transcendentals=300_000),
     )(
-        hidden_in, norm_gain[None, :], w_gate, w_up, w_down, final_gain[None, :], adapter,
+        hidden_in, norm_gain[None, :], w_gate.T, w_up.T, w_down, final_gain[None, :], adapter,
         student_rows, queries, doc_list, teacher_rank,
     )
-    return rows, grad, query, loss[0, 0:1]
+    return pl.pallas_call(
+        hand_over,
+        out_shape=(
+            jax.ShapeDtypeStruct(rows.shape, BF16),
+            jax.ShapeDtypeStruct(grad.shape, F32),
+            jax.ShapeDtypeStruct(query.shape, F32),
+            jax.ShapeDtypeStruct((1,), F32),
+        ),
+        in_specs=[vmem, vmem, vmem, vmem],
+        out_specs=(vmem, vmem, vmem, smem),
+    )(rows, grad, query, loss)
 
 
 def solution(mesh):

time: 92.4 us -> 59.4 us (0.64)
  local copies, waits for them, and re-layouts: 33.3 us -> 0 us
  Pallas kernels: 55.7 us -> 58.4 us
  between operations: 2.41 us -> 0.8 us
    unnamed x5 -> x0, local copies, waits for them, and re-layouts: 33.3 us -> none
    pallas_call x0 -> x1, Pallas kernels: none -> 1.44 us  [fused(): pl.pallas_call(hand_over, out_shape=(jax.ShapeDtypeStruct(rows.shape, BF1...]
    pallas_call x1, Pallas kernels: 55.7 us -> 57 us  [fused(): pl.pallas_call(kernel, out_shape=(jax.ShapeDtypeStruct((4, 5120), BF16),...]
where the time goes in v1:
time: 59.4 us; the launch traced here: 59.2 us
  Pallas kernels  58.4 us (98%)
  between operations  0.8 us (1%)
    pallas_call x1, Pallas kernels, fused(): pl.pallas_call(kernel, out_shape=(jax.ShapeDtypeStruct((4, 5120), BF16),...  57 us
    pallas_call x1, Pallas kernels, fused(): pl.pallas_call(hand_over, out_shape=(jax.ShapeDtypeStruct(rows.shape, BF1...  1.44 us

profile of v1, /device:TPU:0, one launch (start us, length us, event | category | flops | bytes accessed | tf_op | source)
XLA Modules:
  0.0 59.2 jit_solution(17587921743872486555)
XLA Ops:
  0.6 57.0 %shard_map.138 = (bf16[4,5120]{1,0:T(4,128)(2,1)}, f32[4,768]{1,0:T(4,128)}, f32[1,768]{1,0:T(1,128)}, f32[1,128]{1,0:T(1,128)}) custom-call(bf16[16,5120]{1,0:T(8,128)(2,1)} %hin.1, f32[1,5120]{1,0:T(1,128)} %bitcast.6, bf16[1088,5120]{1,0:T(8,128)(2,1)} %bitcast.4, bf16[1088,5120]{1,0:T(8,128)(2,1)} %bitcast.5, bf16[1088,5120]{1,0:T(8,128)(2,1)} %wd_hbm.1, ...), custom_call_target="tpu_custom_call" | custom-call | flops 8000000000 | bytes 34000000 | tf_op jit(solution)/shard_map/pallas_call | solution.py:470
  57.6 1.4 %shard_map.139 = (bf16[4,5120]{1,0:T(4,128)(2,1)}, f32[4,768]{1,0:T(4,128)}, f32[1,768]{1,0:T(1,128)}, f32[1]{0:T(128)}) custom-call(bf16[4,5120]{1,0:T(4,128)(2,1)} %get-tuple-element.8.rows, f32[4,768]{1,0:T(4,128)} %get-tuple-element.9.grad, f32[1,768]{1,0:T(1,128)} %get-tuple-element.10.query, f32[1,128]{1,0:T(1,128)} %get-tuple-element.11.loss), custom_call_target="tpu_custom_call" | custom-call | tf_op jit(solution)/shard_map/pallas_call | solution.py:528

commit v2 on v1

--- a/solution.py
+++ b/solution.py
@@ -225,6 +225,11 @@
         meta = jnp.where((row8 == i) & (lane8 == 1), ranks[i].astype(F32), meta)
     small[0, 5:8, 0:768] = jnp.zeros((3, 768), F32)
     small[0, :, 768:896] = meta
+    small_copies = {}
+    for rel in range(1, CHIPS):
+        dst = slot_of(8 - rel)
+        small_copies[8 - rel] = go(remote(small.at[0], small.at[2 * dst], sm_s.at[rel], sm_r.at[8 - rel], plane(rel)))
+    small_shares = {0: go(remote(small.at[0], small.at[1], sms_s.at[0], sms_r.at[0], sibling))}
 
     def normalise(slot, half):
         rows = block(slot, half)
@@ -299,12 +304,6 @@
     early(*range(4, len(tiles)))
     normalise(7, 0)
     shared(7)
-
-    small_copies = {}
-    for rel in range(1, CHIPS):
-        dst = slot_of(8 - rel)
-        small_copies[8 - rel] = go(remote(small.at[0], small.at[2 * dst], sm_s.at[rel], sm_r.at[8 - rel], plane(rel)))
-    small_shares = {0: go(remote(small.at[0], small.at[1], sms_s.at[0], sms_r.at[0], sibling))}
 
     hidden_rows(FIRST, 256 - FIRST)
 

time: 59.4 us -> 62.8 us (1.057)
  Pallas kernels: 58.4 us -> 61.8 us
    pallas_call x1, Pallas kernels: 57 us -> 60.4 us  [fused(): pl.pallas_call(kernel, out_shape=(jax.ShapeDtypeStruct((4, 5120), BF16),...]
where the time goes in v2:
time: 62.8 us; the launch traced here: 62.6 us
  Pallas kernels  61.8 us (98%)
  between operations  0.8 us (1%)
    pallas_call x1, Pallas kernels, fused(): pl.pallas_call(kernel, out_shape=(jax.ShapeDtypeStruct((4, 5120), BF16),...  60.4 us
    pallas_call x1, Pallas kernels, fused(): pl.pallas_call(hand_over, out_shape=(jax.ShapeDtypeStruct(rows.shape, BF1...  1.44 us

profile of v2, /device:TPU:0, one launch (start us, length us, event | category | flops | bytes accessed | tf_op | source)
XLA Modules:
  0.0 62.6 jit_solution(3421855897812909278)
XLA Ops:
  0.6 60.4 %shard_map.138 = (bf16[4,5120]{1,0:T(4,128)(2,1)}, f32[4,768]{1,0:T(4,128)}, f32[1,768]{1,0:T(1,128)}, f32[1,128]{1,0:T(1,128)}) custom-call(bf16[16,5120]{1,0:T(8,128)(2,1)} %hin.1, f32[1,5120]{1,0:T(1,128)} %bitcast.6, bf16[1088,5120]{1,0:T(8,128)(2,1)} %bitcast.4, bf16[1088,5120]{1,0:T(8,128)(2,1)} %bitcast.5, bf16[1088,5120]{1,0:T(8,128)(2,1)} %wd_hbm.1, ...), custom_call_target="tpu_custom_call" | custom-call | flops 8000000000 | bytes 34000000 | tf_op jit(solution)/shard_map/pallas_call | solution.py:469
  61.0 1.4 %shard_map.139 = (bf16[4,5120]{1,0:T(4,128)(2,1)}, f32[4,768]{1,0:T(4,128)}, f32[1,768]{1,0:T(1,128)}, f32[1]{0:T(128)}) custom-call(bf16[4,5120]{1,0:T(4,128)(2,1)} %get-tuple-element.8.rows, f32[4,768]{1,0:T(4,128)} %get-tuple-element.9.grad, f32[1,768]{1,0:T(1,128)} %get-tuple-element.10.query, f32[1,128]{1,0:T(1,128)} %get-tuple-element.11.loss), custom_call_target="tpu_custom_call" | custom-call | tf_op jit(solution)/shard_map/pallas_call | solution.py:527
